TPU v7x, 512 devices: a whole 4x8x8 slice. The times are simulated.
512 devices in a mesh: ctx: 16 (over y, x_hi), req: 32 (over z, x_lo, core).
Axes of the slice: x: 4 (x_hi: 2, x_lo: 2; x = x_hi * 2 + x_lo), y: 8, z: 8, core: 2. Of those that a mesh axis runs over, the one named last changes fastest.
Arguments:
- queries: bfloat16 [196608, 2048], P(('ctx', 'req')), may hold values from -250 to 250
- suffix_keys: bfloat16 [196608, 512], P(('ctx', 'req')), may hold values from -6 to 6
- suffix_values: bfloat16 [196608, 512], P(('ctx', 'req')), may hold values from -6 to 6
- doc_keys: bfloat16 [2048, 512], P('ctx'), may hold values from -8 to 8
- doc_values: bfloat16 [2048, 512], P('ctx'), may hold values from -6 to 6
- lengths: int32 [1536], P(('ctx', 'req')), may hold values from 1 to 128
- targets: int32 [196608], P(('ctx', 'req')), may hold values from 0 to 31, as said below
Outputs:
- placed: bfloat16 [196608, 2048], P(('ctx', 'req'))
Inputs may be any that keep to these rules, and one draw needn't show every extreme that they name: `targets`: among the 384 slots of each device, every value 0 to 32 - 1 occurs exactly 12 times.
All inputs are finite; a program needn't handle non-finite values.
Results may differ from a plain program's by a relative error of at most 0.013.
Values may be sent and summed in bfloat16 or wider, within the bound.
A program may use at most 128 MiB of HBM per device.

v0:
```python
import math

import jax
import jax.numpy as jnp
from jax import lax
from jax.sharding import PartitionSpec as P

HD = 128
QH = 16
KVH = 4
SUF = 128


def suffix_part(queries, suffix_keys, suffix_values, lengths):
    requests = lengths.shape[0]
    groups = QH // KVH
    factor = 1.0 / math.sqrt(HD)
    query_heads = queries.reshape(requests, SUF, KVH, groups, HD)
    key_heads = suffix_keys.reshape(requests, SUF, KVH, HD)
    value_heads = suffix_values.reshape(requests, SUF, KVH, HD)
    scores = (
        jnp.einsum("rtkgd,rukd->rkgtu", query_heads, key_heads, preferred_element_type=jnp.float32)
        * factor
    )
    causal = jnp.arange(SUF)[:, None] >= jnp.arange(SUF)[None, :]
    scores = jnp.where(causal, scores, -jnp.inf)
    highest = jnp.max(scores, axis=-1)
    weights = jnp.exp(scores - highest[..., None])
    totals = jnp.sum(weights, axis=-1)
    summed = jnp.einsum(
        "rkgtu,rukd->rtkgd",
        weights.astype(jnp.bfloat16),
        value_heads,
        preferred_element_type=jnp.float32,
    )
    normed = summed / jnp.transpose(totals, (0, 3, 1, 2))[..., None]
    log_total = jnp.transpose(highest + jnp.log(totals), (0, 3, 1, 2))
    count_rows = requests * SUF
    live_rows = (
        (jnp.arange(SUF)[None, :] < lengths[:, None]).astype(jnp.float32).reshape(count_rows, 1)
    )
    return (normed.reshape(count_rows, QH * HD), log_total.reshape(count_rows, QH), live_rows)


def doc_part(query_rows, doc_keys, doc_values):
    count_rows = query_rows.shape[0]
    groups = QH // KVH
    factor = 1.0 / math.sqrt(HD)
    query_heads = query_rows.reshape(count_rows, KVH, groups, HD)
    start_state = (
        jnp.full((count_rows, KVH, groups), -jnp.inf, jnp.float32),
        jnp.zeros((count_rows, KVH, groups), jnp.float32),
        jnp.zeros((count_rows, KVH, groups, HD), jnp.float32),
    )
    carry = start_state
    key_piece = lax.all_gather(doc_keys, "ctx", axis=0, tiled=True)
    value_piece = lax.all_gather(doc_values, "ctx", axis=0, tiled=True)
    length = key_piece.shape[0]
    block = math.gcd(length, 256)
    key_blocks = key_piece.reshape(length // block, block, KVH, HD)
    value_blocks = value_piece.reshape(length // block, block, KVH, HD)

    def advance(state, pair):
        highest, totals, summed = state
        key_block, value_block = pair
        scores = (
            jnp.einsum("nkgd,jkd->nkgj", query_heads, key_block, preferred_element_type=jnp.float32)
            * factor
        )
        new_high = jnp.maximum(highest, jnp.max(scores, axis=-1))
        decay = jnp.exp(highest - new_high)
        weights = jnp.exp(scores - new_high[..., None])
        totals = totals * decay + jnp.sum(weights, axis=-1)
        summed = summed * decay[..., None] + jnp.einsum(
            "nkgj,jkd->nkgd",
            weights.astype(jnp.bfloat16),
            value_block,
            preferred_element_type=jnp.float32,
        )
        return ((new_high, totals, summed), None)

    carry, unused = lax.scan(advance, carry, (key_blocks, value_blocks))
    return carry


def combine_parts(normed, log_total, live_rows, state):
    highest, totals, summed = state
    count_rows = highest.shape[0]
    groups = QH // KVH
    log_doc = highest + jnp.log(totals)
    suffix_log = log_total.reshape(count_rows, KVH, groups)
    joint = jnp.logaddexp(suffix_log, log_doc)
    result = jnp.exp(suffix_log - joint)[..., None] * normed.reshape(count_rows, KVH, groups, HD)
    result = result + jnp.exp(highest - joint)[..., None] * summed
    result = result.reshape(count_rows, QH * HD) * live_rows
    return result.astype(jnp.bfloat16)


def body(queries, suffix_keys, suffix_values, doc_keys, doc_values, lengths, targets):
    row_order = jnp.argsort(targets, stable=True)
    normed, log_total, live_rows = suffix_part(queries, suffix_keys, suffix_values, lengths)
    state = doc_part(queries, doc_keys, doc_values)
    finished = combine_parts(normed, log_total, live_rows, state)
    return lax.all_to_all(finished[row_order], "req", split_axis=0, concat_axis=0, tiled=True)


def solution(mesh):
    in_specs = (
        P(("ctx", "req"), None),
        P(("ctx", "req"), None),
        P(("ctx", "req"), None),
        P("ctx", None),
        P("ctx", None),
        P(("ctx", "req")),
        P(("ctx", "req")),
    )
    out_specs = P(("ctx", "req"), None)
    return jax.shard_map(body, mesh=mesh, in_specs=in_specs, out_specs=out_specs, check_vma=False)
```

profile of v0, /device:TPU:1, one launch (start us, length us, event | category | flops | bytes accessed | tf_op | source)
XLA Modules:
  0.0 424.9 jit_solution(8253080963014160194)
XLA Ops:
  8.0 3.8 reshape.49
  31.4 72.1 %all-gather.3.cloned.1.call-done = bf16[2048,512]{1,0:T(8,128)(2,1)} async-done(((bf16[128,512]{1,0:T(8,128)(2,1)}), bf16[2048,512]{1,0:T(8,128)(2,1)}) %all-gather.3.cloned.1.call-update) | async-done | bytes 2097168 | tf_op jit(solution)/shard_map/all_gather | solution.py:56
  103.4 4.0 reshape.69
  107.4 87.0 %all-gather.5.cloned.1.call-done = bf16[2048,512]{1,0:T(8,128)(2,1)} async-done(((bf16[128,512]{1,0:T(8,128)(2,1)}), bf16[2048,512]{1,0:T(8,128)(2,1)}) %all-gather.5.cloned.1.call-update) | async-done | bytes 2097168 | tf_op jit(solution)/shard_map/all_gather | solution.py:57
  194.4 4.0 reshape.70
  198.4 134.7 %while.15 = (s32[]{:T(128)}, f32[384,4,4]{0,2,1:T(4,128)S(1)}, f32[384,4,4]{0,2,1:T(4,128)S(1)}, f32[384,4,4,128]{0,3,2,1:T(8,128)S(1)}, bf16[8,256,4,128]{3,2,1...) while((s32[]{:T(128)}, f32[384,4,4]{0,2,1:T(4,128)S(1)}, ...), condition=%wide.region_5.6_spmd.clone, body=%wide.region_2.0_spmd.clone.sunk | while | flops 820279296 | bytes 29229164 | solution.py:82
  200.3 5.1 %bitcast_reduce_fusion.2 = (f32[384,4,4]{0,2,1:T(4,128)S(1)}, f32[4,256,384,4]{2,1,3,0:T(8,128)}) fusion(bf16[384,4,4,128]{3,0,2,1:T(8,128)(2,1)} %get-tuple-element.189, bf16[1,256,4,128]{3,2,1,0:T(4,128)(2,1)S(1)} %get-tuple-element.160), kind=kOutput, calls=%fused_computation.2.clone.1 | convolution fusion | flops 405792768 | bytes 8151040 | tf_op jit(solution)/shard_map/while/body/eval_jaxpr/nkgd,jkd->nkgj/dot_general | solution.py:67
  205.4 3.9 fusion.42
  210.4 4.8 %bitcast_add_fusion.4 = f32[384,4,4,128]{0,3,2,1:T(8,128)S(1)} fusion(f32[384,4,4,128]{0,3,2,1:T(8,128)S(1)} %get-tuple-element.178, f32[4,256,384,4]{2,1,3,0:T(8,128)} %get-tuple-element.162, f32[384,4,4]{0,2,1:T(4,128)S(1)} %select_maximum_fusion.2, f32[384,4,4]{0,2,1:T(4,128)S(1)} %get-tuple-element.164, pred[]{:T(512)S(6)} %compare.7, ...), kind=kOutput, calls=%fused_computation.7.clone.1 | convolution fusion | flops 409731072 | bytes 12894209 | tf_op jit(solution)/shard_map/while/body/eval_jaxpr/nkgj,jkd->nkgd/dot_general | solution.py:74
  217.2 5.1 %bitcast_reduce_fusion.2 = (f32[384,4,4]{0,2,1:T(4,128)S(1)}, f32[4,256,384,4]{2,1,3,0:T(8,128)}) fusion(bf16[384,4,4,128]{3,0,2,1:T(8,128)(2,1)} %get-tuple-element.189, bf16[1,256,4,128]{3,2,1,0:T(4,128)(2,1)S(1)} %get-tuple-element.160), kind=kOutput, calls=%fused_computation.2.clone.1 | convolution fusion | flops 405792768 | bytes 8151040 | tf_op jit(solution)/shard_map/while/body/eval_jaxpr/nkgd,jkd->nkgj/dot_general | solution.py:67
  222.2 3.9 fusion.42
  227.2 4.8 %bitcast_add_fusion.4 = f32[384,4,4,128]{0,3,2,1:T(8,128)S(1)} fusion(f32[384,4,4,128]{0,3,2,1:T(8,128)S(1)} %get-tuple-element.178, f32[4,256,384,4]{2,1,3,0:T(8,128)} %get-tuple-element.162, f32[384,4,4]{0,2,1:T(4,128)S(1)} %select_maximum_fusion.2, f32[384,4,4]{0,2,1:T(4,128)S(1)} %get-tuple-element.164, pred[]{:T(512)S(6)} %compare.7, ...), kind=kOutput, calls=%fused_computation.7.clone.1 | convolution fusion | flops 409731072 | bytes 12894209 | tf_op jit(solution)/shard_map/while/body/eval_jaxpr/nkgj,jkd->nkgd/dot_general | solution.py:74
  234.0 5.1 %bitcast_reduce_fusion.2 = (f32[384,4,4]{0,2,1:T(4,128)S(1)}, f32[4,256,384,4]{2,1,3,0:T(8,128)}) fusion(bf16[384,4,4,128]{3,0,2,1:T(8,128)(2,1)} %get-tuple-element.189, bf16[1,256,4,128]{3,2,1,0:T(4,128)(2,1)S(1)} %get-tuple-element.160), kind=kOutput, calls=%fused_computation.2.clone.1 | convolution fusion | flops 405792768 | bytes 8151040 | tf_op jit(solution)/shard_map/while/body/eval_jaxpr/nkgd,jkd->nkgj/dot_general | solution.py:67
  239.1 3.9 fusion.42
  244.1 4.8 %bitcast_add_fusion.4 = f32[384,4,4,128]{0,3,2,1:T(8,128)S(1)} fusion(f32[384,4,4,128]{0,3,2,1:T(8,128)S(1)} %get-tuple-element.178, f32[4,256,384,4]{2,1,3,0:T(8,128)} %get-tuple-element.162, f32[384,4,4]{0,2,1:T(4,128)S(1)} %select_maximum_fusion.2, f32[384,4,4]{0,2,1:T(4,128)S(1)} %get-tuple-element.164, pred[]{:T(512)S(6)} %compare.7, ...), kind=kOutput, calls=%fused_computation.7.clone.1 | convolution fusion | flops 409731072 | bytes 12894209 | tf_op jit(solution)/shard_map/while/body/eval_jaxpr/nkgj,jkd->nkgd/dot_general | solution.py:74
  250.9 5.1 %bitcast_reduce_fusion.2 = (f32[384,4,4]{0,2,1:T(4,128)S(1)}, f32[4,256,384,4]{2,1,3,0:T(8,128)}) fusion(bf16[384,4,4,128]{3,0,2,1:T(8,128)(2,1)} %get-tuple-element.189, bf16[1,256,4,128]{3,2,1,0:T(4,128)(2,1)S(1)} %get-tuple-element.160), kind=kOutput, calls=%fused_computation.2.clone.1 | convolution fusion | flops 405792768 | bytes 8151040 | tf_op jit(solution)/shard_map/while/body/eval_jaxpr/nkgd,jkd->nkgj/dot_general | solution.py:67
  255.9 3.9 fusion.42
  260.9 4.8 %bitcast_add_fusion.4 = f32[384,4,4,128]{0,3,2,1:T(8,128)S(1)} fusion(f32[384,4,4,128]{0,3,2,1:T(8,128)S(1)} %get-tuple-element.178, f32[4,256,384,4]{2,1,3,0:T(8,128)} %get-tuple-element.162, f32[384,4,4]{0,2,1:T(4,128)S(1)} %select_maximum_fusion.2, f32[384,4,4]{0,2,1:T(4,128)S(1)} %get-tuple-element.164, pred[]{:T(512)S(6)} %compare.7, ...), kind=kOutput, calls=%fused_computation.7.clone.1 | convolution fusion | flops 409731072 | bytes 12894209 | tf_op jit(solution)/shard_map/while/body/eval_jaxpr/nkgj,jkd->nkgd/dot_general | solution.py:74
  267.7 5.1 %bitcast_reduce_fusion.2 = (f32[384,4,4]{0,2,1:T(4,128)S(1)}, f32[4,256,384,4]{2,1,3,0:T(8,128)}) fusion(bf16[384,4,4,128]{3,0,2,1:T(8,128)(2,1)} %get-tuple-element.189, bf16[1,256,4,128]{3,2,1,0:T(4,128)(2,1)S(1)} %get-tuple-element.160), kind=kOutput, calls=%fused_computation.2.clone.1 | convolution fusion | flops 405792768 | bytes 8151040 | tf_op jit(solution)/shard_map/while/body/eval_jaxpr/nkgd,jkd->nkgj/dot_general | solution.py:67
  272.8 3.9 fusion.42
  277.8 4.8 %bitcast_add_fusion.4 = f32[384,4,4,128]{0,3,2,1:T(8,128)S(1)} fusion(f32[384,4,4,128]{0,3,2,1:T(8,128)S(1)} %get-tuple-element.178, f32[4,256,384,4]{2,1,3,0:T(8,128)} %get-tuple-element.162, f32[384,4,4]{0,2,1:T(4,128)S(1)} %select_maximum_fusion.2, f32[384,4,4]{0,2,1:T(4,128)S(1)} %get-tuple-element.164, pred[]{:T(512)S(6)} %compare.7, ...), kind=kOutput, calls=%fused_computation.7.clone.1 | convolution fusion | flops 409731072 | bytes 12894209 | tf_op jit(solution)/shard_map/while/body/eval_jaxpr/nkgj,jkd->nkgd/dot_general | solution.py:74
  284.5 5.1 %bitcast_reduce_fusion.2 = (f32[384,4,4]{0,2,1:T(4,128)S(1)}, f32[4,256,384,4]{2,1,3,0:T(8,128)}) fusion(bf16[384,4,4,128]{3,0,2,1:T(8,128)(2,1)} %get-tuple-element.189, bf16[1,256,4,128]{3,2,1,0:T(4,128)(2,1)S(1)} %get-tuple-element.160), kind=kOutput, calls=%fused_computation.2.clone.1 | convolution fusion | flops 405792768 | bytes 8151040 | tf_op jit(solution)/shard_map/while/body/eval_jaxpr/nkgd,jkd->nkgj/dot_general | solution.py:67
  289.6 3.9 fusion.42
  294.6 4.8 %bitcast_add_fusion.4 = f32[384,4,4,128]{0,3,2,1:T(8,128)S(1)} fusion(f32[384,4,4,128]{0,3,2,1:T(8,128)S(1)} %get-tuple-element.178, f32[4,256,384,4]{2,1,3,0:T(8,128)} %get-tuple-element.162, f32[384,4,4]{0,2,1:T(4,128)S(1)} %select_maximum_fusion.2, f32[384,4,4]{0,2,1:T(4,128)S(1)} %get-tuple-element.164, pred[]{:T(512)S(6)} %compare.7, ...), kind=kOutput, calls=%fused_computation.7.clone.1 | convolution fusion | flops 409731072 | bytes 12894209 | tf_op jit(solution)/shard_map/while/body/eval_jaxpr/nkgj,jkd->nkgd/dot_general | solution.py:74
  301.4 5.1 %bitcast_reduce_fusion.2 = (f32[384,4,4]{0,2,1:T(4,128)S(1)}, f32[4,256,384,4]{2,1,3,0:T(8,128)}) fusion(bf16[384,4,4,128]{3,0,2,1:T(8,128)(2,1)} %get-tuple-element.189, bf16[1,256,4,128]{3,2,1,0:T(4,128)(2,1)S(1)} %get-tuple-element.160), kind=kOutput, calls=%fused_computation.2.clone.1 | convolution fusion | flops 405792768 | bytes 8151040 | tf_op jit(solution)/shard_map/while/body/eval_jaxpr/nkgd,jkd->nkgj/dot_general | solution.py:67
  306.5 3.9 fusion.42
  311.5 4.8 %bitcast_add_fusion.4 = f32[384,4,4,128]{0,3,2,1:T(8,128)S(1)} fusion(f32[384,4,4,128]{0,3,2,1:T(8,128)S(1)} %get-tuple-element.178, f32[4,256,384,4]{2,1,3,0:T(8,128)} %get-tuple-element.162, f32[384,4,4]{0,2,1:T(4,128)S(1)} %select_maximum_fusion.2, f32[384,4,4]{0,2,1:T(4,128)S(1)} %get-tuple-element.164, pred[]{:T(512)S(6)} %compare.7, ...), kind=kOutput, calls=%fused_computation.7.clone.1 | convolution fusion | flops 409731072 | bytes 12894209 | tf_op jit(solution)/shard_map/while/body/eval_jaxpr/nkgj,jkd->nkgd/dot_general | solution.py:74
  318.2 5.1 %bitcast_reduce_fusion.2 = (f32[384,4,4]{0,2,1:T(4,128)S(1)}, f32[4,256,384,4]{2,1,3,0:T(8,128)}) fusion(bf16[384,4,4,128]{3,0,2,1:T(8,128)(2,1)} %get-tuple-element.189, bf16[1,256,4,128]{3,2,1,0:T(4,128)(2,1)S(1)} %get-tuple-element.160), kind=kOutput, calls=%fused_computation.2.clone.1 | convolution fusion | flops 405792768 | bytes 8151040 | tf_op jit(solution)/shard_map/while/body/eval_jaxpr/nkgd,jkd->nkgj/dot_general | solution.py:67
  323.3 3.9 fusion.42
  328.3 4.8 %bitcast_add_fusion.4 = f32[384,4,4,128]{0,3,2,1:T(8,128)S(1)} fusion(f32[384,4,4,128]{0,3,2,1:T(8,128)S(1)} %get-tuple-element.178, f32[4,256,384,4]{2,1,3,0:T(8,128)} %get-tuple-element.162, f32[384,4,4]{0,2,1:T(4,128)S(1)} %select_maximum_fusion.2, f32[384,4,4]{0,2,1:T(4,128)S(1)} %get-tuple-element.164, pred[]{:T(512)S(6)} %compare.7, ...), kind=kOutput, calls=%fused_computation.7.clone.1 | convolution fusion | flops 409731072 | bytes 12894209 | tf_op jit(solution)/shard_map/while/body/eval_jaxpr/nkgj,jkd->nkgd/dot_general | solution.py:74
  335.6 4.5 %fusion.13 = f32[384,4,4,128]{3,0,2,1:T(8,128)S(1)} fusion(f32[3,128,4,4,128]{4,1,0,3,2:T(8,128)} %copy.43, f32[384,4,4,128]{3,0,2,1:T(8,128)} %copy.44, f32[384,4,4]{0,2,1:T(4,128)S(1)} %get-tuple-element.108, f32[384,4,4]{0,2,1:T(4,128)S(1)} %get-tuple-element.107), kind=kLoop, calls=%fused_computation.22 | loop fusion | flops 2359296 | bytes 9486336 | tf_op jit(solution)/shard_map/add | solution.py:94
  352.6 61.9 %all_to_all.12 = bf16[32,12,2048]{2,1,0:T(8,128)(2,1)} all-to-all(bf16[32,12,2048]{2,1,0:T(8,128)(2,1)S(1)} %all_to_all.8), channel_id=1, replica_groups=mesh['ctx'=16,'req'=32] {'req'}, dimensions={0} | all-to-all | bytes 3145728 | tf_op jit(solution)/shard_map/all_to_all | solution.py:104
  (81 shorter events, 63.9 us)
Async XLA Ops:
  6.5 5.3 %copy-start = (bf16[384,2048]{1,0:T(8,128)(2,1)S(1)}, bf16[384,2048]{1,0:T(8,128)(2,1)}, u32[]{:S(2)}) copy-start(bf16[384,2048]{1,0:T(8,128)(2,1)} %param.9) | copy-start | bytes 4718596
  6.5 96.9 %all-gather.3.cloned.1.call-start = ((), (), s32[]{:S(2)}) async-start(), calls=%async_computation.1 | async-start | bytes 2228224 | tf_op jit(solution)/shard_map/all_gather | solution.py:56
  7.3 187.2 %all-gather.5.cloned.1.call-start = ((), (), s32[]{:S(2)}) async-start(), calls=%async_computation.2 | async-start | bytes 2228224 | tf_op jit(solution)/shard_map/all_gather | solution.py:57
  17.1 3.1 copy-start.1
  23.7 2.6 copy-start.4
  23.7 7.0 %copy-start.5 = (s32[3]{0:T(128)S(1)}, s32[3]{0:T(128)}, u32[]{:S(2)}) copy-start(s32[3]{0:T(128)} %param.14) | copy-start | bytes 40
  342.1 2.8 copy-start.3
  345.0 2.1 copy-start.2
Sparse Core Ops, SparseCore 0:
  10.5 92.8 all-gather.2
  106.6 87.7 all-gather.4
where the time goes:
time: 427 us; the launch traced here: 425 us
  waiting for transfers between devices  160 us (37%)
  matrix products  83 us (19%)
  local copies, waits for them, and re-layouts  62 us (15%)
  blocking collectives  61.9 us (14%)
  other arithmetic  43.7 us (10%)
  between operations  13.5 us (3%)
    all_gather x1, waiting for transfers between devices, doc_part(): value_piece = lax.all_gather(doc_values, 'ctx', axis=0, tiled=True)  87 us
    all_gather x1, waiting for transfers between devices, doc_part(): key_piece = lax.all_gather(doc_keys, 'ctx', axis=0, tiled=True)  72.1 us
    all_to_all x1, blocking collectives, body(): lax.all_to_all(finished[row_order], 'req', split_axis=0, concat_axis=0, t...  61.9 us
    dot_general x8, matrix products, advance(): jnp.einsum('nkgd,jkd->nkgj', query_heads, key_block, preferred_element_ty...  40.5 us
    dot_general x8, matrix products, advance(): jnp.einsum('nkgj,jkd->nkgd', weights.astype(jnp.bfloat16), value_block, p...  38.6 us
    reduce_sum x8, other arithmetic, advance(): totals = totals * decay + jnp.sum(weights, axis=-1)  30.8 us
    dynamic_slice x16, local copies, waits for them, and re-layouts, doc_part(): carry, unused = lax.scan(advance, carry, (key_blocks, value_blocks))  24.1 us
  transfers between devices with their start and end apart: 2, of which 2 were waited for; matrix products, arithmetic and copies ran while one was open for 6% of the time, Pallas kernels for 0%

commit v1 on v0

v1 whole, which is shorter than its diff:
```python
import math

import jax
import jax.numpy as jnp
from jax import lax
from jax.experimental import pallas as pl
from jax.experimental.pallas import tpu as pltpu
from jax.sharding import PartitionSpec as P

HD = 128
KVH = 4
GROUPS = 4
SUF = 128
REQ_DEV = 3
TOK = 384
N_REQ = 32
PER = 12
TILE = 16
Y = 8
HALF = 64
SCALE = math.log2(math.e) / math.sqrt(HD)
NT = (((1,), (1,)), ((), ()))
MESH = pl.DeviceIdType.MESH
F32 = jnp.float32
BF16 = jnp.bfloat16
BLOCKS = ((0, 1), (1, 3), (3, 5), (5, 7), (7, 8))


def kernel(
    q_ref, sk_ref, sv_ref, dk_ref, dv_ref, len_ref, tgt_ref, out_ref,
    kv, vt, high, total, acc, res, pick, unpick, send, recv,
    ring_send, ring_recv, core_recv, ex_send, ex_recv,
):
    ctx, req = lax.axis_index("ctx"), lax.axis_index("req")
    y, xh = ctx // 2, ctx % 2
    z, quad = req // 4, req % 4
    xl, core = quad // 2, quad % 2
    up = ((y + 1) % Y) * 2 + xh
    down = ((y + Y - 1) % Y) * 2 + xh
    across = y * 2 + 1 - xh
    twin = req + 1 - 2 * core

    barrier = pltpu.get_barrier_semaphore()
    for other in (up, down, across):
        pl.semaphore_signal(barrier, inc=1, device_id=(other, req), device_id_type=MESH)

    @pl.loop(1, N_REQ)
    def _(s):
        pl.semaphore_signal(
            barrier, inc=1, device_id=(ctx, (req + s) % N_REQ), device_id_type=MESH
        )

    for g in range(KVH):
        lanes = slice(g * HD, (g + 1) * HD)
        for hf in range(2):
            start = core * HALF if hf == 0 else (1 - core) * HALF
            rows = pl.ds(pl.multiple_of(start, HALF), HALF)
            kv[0, g, 0, 0, hf] = dk_ref[rows, lanes]
            kv[1, g, 0, 0, hf] = dv_ref[rows, lanes]

    def ring(g, src, dst, st, other):
        pltpu.make_async_remote_copy(
            kv.at[:, g, src, st, 0], kv.at[:, g, dst, st, 0],
            ring_send.at[g], ring_recv.at[g, dst, st],
            device_id=(other, req), device_id_type=MESH,
        ).start()

    def pass_on(g, pos, st):
        pltpu.make_async_remote_copy(
            kv.at[:, g, pos, st, 0], kv.at[:, g, pos, st, 1],
            ring_send.at[g], core_recv.at[g, pos, st],
            device_id=(ctx, twin), device_id_type=MESH,
        ).start()

    def arrived(g, pos, st):
        part = kv.at[:, g, pos, st, 0]
        pltpu.make_async_copy(part, part, ring_recv.at[g, pos, st]).wait()

    def passed(g, pos, st):
        part = kv.at[:, g, pos, st, 1]
        pltpu.make_async_copy(part, part, core_recv.at[g, pos, st]).wait()

    def ring_start(g):
        ring(g, 0, 1, 0, up)
        ring(g, 0, 2, 0, down)
        pltpu.make_async_remote_copy(
            kv.at[:, g, 0, 0, 0], kv.at[:, g, 0, 1, 0],
            ring_send.at[g], ring_recv.at[g, 0, 1],
            device_id=(across, req), device_id_type=MESH,
        ).start()

    def ring_second(g):
        arrived(g, 0, 1)
        ring(g, 0, 1, 1, up)
        ring(g, 0, 2, 1, down)
        pass_on(g, 0, 1)

    def ring_stage(g, k):
        for st in range(2):
            if k == 4:
                arrived(g, 7, st)
                pass_on(g, 7, st)
                continue
            arrived(g, 2 * k - 1, st)
            if k < 3 or st == 0:
                ring(g, 2 * k - 1, 2 * k + 1, st, up)
            pass_on(g, 2 * k - 1, st)
            arrived(g, 2 * k, st)
            if k < 3:
                ring(g, 2 * k, 2 * k + 2, st, down)
            elif st == 1:
                ring(g, 2 * k, 7, st, down)
            pass_on(g, 2 * k, st)

    def whole(g, first, last):
        for pos in range(first, last):
            for st in range(2):
                if pos > 0 or st > 0:
                    passed(g, pos, st)

    def query(g, hh):
        return q_ref[:, pl.ds(pl.multiple_of((g * GROUPS + hh) * HD, HD), HD)]

    lower = lax.broadcasted_iota(jnp.int32, (SUF, SUF), 0) <= lax.broadcasted_iota(
        jnp.int32, (SUF, SUF), 1
    )

    def suffix(g, hh):
        q = query(g, hh)
        lanes = pl.ds(pl.multiple_of(g * HD, HD), HD)
        for r in range(REQ_DEV):
            rows = slice(r * SUF, (r + 1) * SUF)
            s = lax.dot_general(sk_ref[rows, lanes], q[rows], NT, preferred_element_type=F32)
            s = jnp.where(lower, s, -jnp.inf)
            top = jnp.max(s, axis=0, keepdims=True)
            p = jnp.exp2((s - top) * SCALE)
            high[hh, :, rows] = top
            total[hh, :, rows] = jnp.sum(p, axis=0, keepdims=True)
            acc[hh, :, rows] = jnp.dot(
                sv_ref[rows, lanes].T, p.astype(BF16), preferred_element_type=F32
            )

    def turn(g, first, last):
        n = (last - first) * 256
        v = kv[1, g, first:last].reshape(n, HD)
        vt[:, first * 256 : last * 256] = v.T

    def update(g, hh, first, last):
        n = (last - first) * 256
        keys = kv[0, g, first:last].reshape(n, HD)
        s = lax.dot_general(keys, query(g, hh), NT, preferred_element_type=F32)
        old = high[hh]
        top = jnp.maximum(old, jnp.max(s, axis=0, keepdims=True))
        decay = jnp.exp2((old - top) * SCALE)
        p = jnp.exp2((s - top) * SCALE)
        high[hh] = top
        total[hh] = total[hh] * decay + jnp.sum(p, axis=0, keepdims=True)
        acc[hh] = acc[hh] * decay + jnp.dot(
            vt[:, first * 256 : last * 256], p.astype(BF16), preferred_element_type=F32
        )

    lane = lax.broadcasted_iota(jnp.int32, (1, SUF), 1)
    live = jnp.concatenate([(lane < len_ref[r]).astype(F32) for r in range(REQ_DEV)], axis=1)

    def finish(hh):
        o = acc[hh] * (1.0 / total[hh])
        res[hh] = jnp.where(live > 0.0, o, 0.0).astype(BF16)

    def dispatch(g):
        for j in range(3):
            t = lax.dot_general(pick[0], res[j], NT, preferred_element_type=F32)
            t += lax.dot_general(pick[1 + j], res[3], NT, preferred_element_type=F32)
            send[g, :, j] = t.astype(BF16).reshape(N_REQ, TILE, HD)
        pltpu.make_async_copy(send.at[g, req], recv.at[g, req], ex_recv.at[g]).start()

        @pl.loop(0, N_REQ - 1)
        def _(s):
            j = s // 4
            step = (j // 2 + 1) * (1 - 2 * (j % 2)) + 4 * (j // 7)
            turned = s % 4 + s // 28
            x2, c2 = (xl + turned // 2) % 2, (core + turned) % 2
            dest = ((z + step + 8) % 8) * 4 + x2 * 2 + c2
            pltpu.make_async_remote_copy(
                send.at[g, dest], recv.at[g, req], ex_send.at[g], ex_recv.at[g],
                device_id=(ctx, dest), device_id_type=MESH,
            ).start()

    def collect(g):
        pltpu.make_async_copy(recv.at[g], recv.at[g], ex_recv.at[g]).wait()
        tiles = [recv[g, :, j].reshape(N_REQ * TILE, HD) for j in range(3)]
        last = None
        for j in range(3):
            lanes = slice((g * GROUPS + j) * HD, (g * GROUPS + j + 1) * HD)
            out_ref[:, lanes] = jnp.dot(unpick[0], tiles[j], preferred_element_type=F32).astype(BF16)
            t = jnp.dot(unpick[1 + j], tiles[j], preferred_element_type=F32)
            last = t if last is None else last + t
        out_ref[:, (g * GROUPS + 3) * HD : (g * GROUPS + 4) * HD] = last.astype(BF16)

    tgt = tgt_ref[...].reshape(1, TOK)
    mine = lax.broadcasted_iota(jnp.int32, (N_REQ, TOK), 0) == tgt
    before = lax.broadcasted_iota(jnp.int32, (TOK, TOK), 0) < lax.broadcasted_iota(
        jnp.int32, (TOK, TOK), 1
    )
    counts = jnp.dot(
        mine.astype(F32).astype(BF16), before.astype(F32).astype(BF16), preferred_element_type=F32
    )
    rank = jnp.sum(jnp.where(mine, counts, 0.0), axis=0, keepdims=True).astype(jnp.int32)
    row = lax.broadcasted_iota(jnp.int32, (N_REQ * TILE, TOK), 0)
    pick[0] = (row == tgt * TILE + rank).astype(F32).astype(BF16)
    spot = lax.broadcasted_iota(jnp.int32, (TOK, N_REQ * TILE), 1)
    place = lax.broadcasted_iota(jnp.int32, (TOK, N_REQ * TILE), 0)
    source, k = spot // TILE, spot % TILE
    unpick[0] = jnp.logical_and(place == source * PER + k, k < PER).astype(F32).astype(BF16)
    for j in range(3):
        inside = jnp.logical_and(rank >= 4 * j, rank < 4 * j + 4)
        code = jnp.where(inside, tgt * TILE + PER + rank - 4 * j, -1)
        pick[1 + j] = (row == code).astype(F32).astype(BF16)
        unpick[1 + j] = (
            jnp.logical_and(place == source * PER + 4 * j + k - PER, k >= PER)
            .astype(F32)
            .astype(BF16)
        )

    pl.semaphore_wait(barrier, N_REQ + 2)

    ring_start(0)

    @pl.loop(0, GROUPS)
    def _(hh):
        suffix(0, hh)

    ring_second(0)
    for k, (first, last) in enumerate(BLOCKS):
        if k < 4:
            ring_stage(0, k + 1)
        if k == 2:
            ring_start(1)
        if k == 3:
            ring_second(1)
            ring_stage(1, 1)
        if k == 4:
            ring_stage(1, 2)
        whole(0, first, last)
        turn(0, first, last)

        @pl.loop(0, GROUPS)
        def _(hh):
            update(0, hh, first, last)

    @pl.loop(0, GROUPS)
    def _(hh):
        finish(hh)

    dispatch(0)
    ring_stage(1, 3)

    @pl.loop(0, GROUPS)
    def _(hh):
        suffix(1, hh)

    ring_stage(1, 4)

    @pl.loop(1, KVH)
    def _(g):
        whole(g, 0, 8)
        turn(g, 0, 8)

        @pl.loop(0, GROUPS)
        def _(hh):
            @pl.when(g < KVH - 1)
            def _():
                @pl.when(hh == 0)
                def _():
                    ring_start(g + 1)

                @pl.when(hh == 1)
                def _():
                    ring_second(g + 1)
                    ring_stage(g + 1, 1)

                @pl.when(hh == 2)
                def _():
                    ring_stage(g + 1, 2)

                @pl.when(hh == 3)
                def _():
                    ring_stage(g + 1, 3)

            @pl.when(g > 1)
            def _():
                suffix(g, hh)

            update(g, hh, 0, 8)
            finish(hh)

        dispatch(g)

        @pl.when(g < KVH - 1)
        def _():
            ring_stage(g + 1, 4)

    for g in range(KVH):
        collect(g)
    for g in range(KVH):
        out = send.at[g, 0 : N_REQ - 1]
        pltpu.make_async_copy(out, out, ex_send.at[g]).wait()
        left = kv.at[:, 0:3, 0:5, :, 0]
        pltpu.make_async_copy(left, left, ring_send.at[g]).wait()


def body(queries, suffix_keys, suffix_values, doc_keys, doc_values, lengths, targets):
    vmem = pl.BlockSpec(memory_space=pltpu.VMEM)
    return pl.pallas_call(
        kernel,
        out_shape=jax.ShapeDtypeStruct((TOK, KVH * GROUPS * HD), BF16),
        in_specs=[vmem] * 5 + [pl.BlockSpec(memory_space=pltpu.SMEM), vmem],
        out_specs=vmem,
        scratch_shapes=[
            pltpu.VMEM((2, KVH, Y, 2, 2, HALF, HD), BF16),
            pltpu.VMEM((HD, Y * 256), BF16),
            pltpu.VMEM((GROUPS, 1, TOK), F32),
            pltpu.VMEM((GROUPS, 1, TOK), F32),
            pltpu.VMEM((GROUPS, HD, TOK), F32),
            pltpu.VMEM((GROUPS, HD, TOK), BF16),
            pltpu.VMEM((4, N_REQ * TILE, TOK), BF16),
            pltpu.VMEM((4, TOK, N_REQ * TILE), BF16),
            pltpu.VMEM((KVH, N_REQ, 3, TILE, HD), BF16),
            pltpu.VMEM((KVH, N_REQ, 3, TILE, HD), BF16),
            pltpu.SemaphoreType.DMA((KVH,)),
            pltpu.SemaphoreType.DMA((KVH, Y, 2)),
            pltpu.SemaphoreType.DMA((KVH, Y, 2)),
            pltpu.SemaphoreType.DMA((KVH,)),
            pltpu.SemaphoreType.DMA((KVH,)),
        ],
        compiler_params=pltpu.CompilerParams(
            collective_id=0, has_side_effects=True, vmem_limit_bytes=48 << 20
        ),
        cost_estimate=pl.CostEstimate(
            flops=7_000_000_000, bytes_accessed=4_000_000, transcendentals=13_000_000
        ),
    )(queries, suffix_keys, suffix_values, doc_keys, doc_values, lengths, targets)


def solution(mesh):
    both = P(("ctx", "req"), None)
    flat = P(("ctx", "req"))
    in_specs = (both, both, both, P("ctx", None), P("ctx", None), flat, flat)
    return jax.shard_map(body, mesh=mesh, in_specs=in_specs, out_specs=both, check_vma=False)
```

time: 427 us -> 118 us (0.28)
  waiting for transfers between devices: 160 us -> 0 us
  Pallas kernels: 0 us -> 109 us
  matrix products: 83 us -> 0 us
  blocking collectives: 61.9 us -> 0 us
  local copies, waits for them, and re-layouts: 62 us -> 7.69 us
  other arithmetic: 43.7 us -> 0 us
  between operations: 13.5 us -> 0.02 us
    all_gather x2 -> x0, waiting for transfers between devices: 159 us -> none  [the longest x1 87 us: doc_part(): value_piece = lax.all_gather(doc_values, 'ctx', axis=0, tiled=True)]
    pallas_call x0 -> x1, Pallas kernels: none -> 109 us  [body(): pl.pallas_call(kernel, out_shape=jax.ShapeDtypeStruct((TOK, KVH * GROUPS...]
    dot_general x18 -> x0, matrix products: 83 us -> none  [the longest x8 40.5 us: advance(): jnp.einsum('nkgd,jkd->nkgj', query_heads, key_block, preferred_element_ty...]
    all_to_all x1 -> x0, blocking collectives: 61.9 us -> none  [body(): lax.all_to_all(finished[row_order], 'req', split_axis=0, concat_axis=0, t...]
    reduce_sum x9 -> x0, other arithmetic: 31.6 us -> none  [the longest x8 30.8 us: advance(): totals = totals * decay + jnp.sum(weights, axis=-1)]
    dynamic_slice x16 -> x0, local copies, waits for them, and re-layouts: 24.1 us -> none  [doc_part(): carry, unused = lax.scan(advance, carry, (key_blocks, value_blocks))]
    reshape x6 -> x0, local copies, waits for them, and re-layouts: 18.3 us -> none  [the longest x1 4.01 us: doc_part(): value_blocks = value_piece.reshape(length // block, block, KVH, HD)]
    all_to_all x2 -> x0, local copies, waits for them, and re-layouts: 5.97 us -> none  [body(): lax.all_to_all(finished[row_order], 'req', split_axis=0, concat_axis=0, t...]
  transfers between devices with their start and end apart: 2 -> 0, of which waited for: 2 -> 0; matrix products, arithmetic and copies ran while one was open for 6% -> 0% of each run, Pallas kernels for 0% -> 0%
where the time goes in v1:
time: 118 us; the launch traced here: 117 us
  Pallas kernels  109 us (92%)
  local copies, waits for them, and re-layouts  7.69 us (7%)
    pallas_call x1, Pallas kernels, body(): pl.pallas_call(kernel, out_shape=jax.ShapeDtypeStruct((TOK, KVH * GROUPS...  109 us
    unnamed x15, local copies, waits for them, and re-layouts  7.69 us

profile of v1, /device:TPU:1, one launch (start us, length us, event | category | flops | bytes accessed | tf_op | source)
XLA Modules:
  0.0 116.8 jit_solution(4465093552001748685)
XLA Ops:
  0.0 0.0 copy-start
  0.0 1.4 %copy-done = bf16[384,2048]{1,0:T(8,128)(2,1)S(1)} copy-done((bf16[384,2048]{1,0:T(8,128)(2,1)S(1)}, bf16[384,2048]{1,0:T(8,128)(2,1)}, u32[]{:S(2)}) %copy-start) | copy-done | bytes 1572888
  1.4 0.0 copy-start.1
  1.4 1.0 copy-done.1
  2.4 0.0 copy-start.2
  2.4 1.0 copy-done.2
  3.4 0.0 copy-start.3
  3.4 0.9 copy-done.3
  4.3 0.0 copy-start.4
  4.3 0.9 copy-done.4
  5.2 0.0 copy-start.5
  5.2 0.7 copy-done.5
  5.9 0.0 copy-start.6
  5.9 0.7 copy-done.6
  6.5 109.1 %shard_map.73 = bf16[384,2048]{1,0:T(8,128)(2,1)S(1)} custom-call(bf16[384,2048]{1,0:T(8,128)(2,1)S(1)} %copy-done, bf16[384,512]{1,0:T(8,128)(2,1)S(1)} %copy-done.1, bf16[384,512]{1,0:T(8,128)(2,1)S(1)} %copy-done.2, bf16[128,512]{1,0:T(8,128)(2,1)S(1)} %copy-done.3, bf16[128,512]{1,0:T(8,128)(2,1)S(1)} %copy-done.4, s32[3]{0:T(128)S(1)} %copy-done.6, ...), custom_call_target="tpu_custom_call" | custom-call | flops 7000000000 | bytes 4000000 | tf_op jit(solution)/shard_map/pallas_call | solution.py:313
  115.7 1.1 copy.9
Async XLA Ops:
  0.0 1.4 %copy-start = (bf16[384,2048]{1,0:T(8,128)(2,1)S(1)}, bf16[384,2048]{1,0:T(8,128)(2,1)}, u32[]{:S(2)}) copy-start(bf16[384,2048]{1,0:T(8,128)(2,1)} %q_ref.1) | copy-start | bytes 4718596
  1.4 1.0 copy-start.1
  2.4 1.0 copy-start.2
  3.4 0.9 copy-start.3
  4.3 0.9 copy-start.4
  5.2 0.7 copy-start.5
  5.9 0.7 copy-start.6

commit v2 on v1

v2 whole, which is shorter than its diff:
```python
import math

import jax
import jax.numpy as jnp
from jax import lax
from jax.experimental import pallas as pl
from jax.experimental.pallas import tpu as pltpu
from jax.sharding import PartitionSpec as P

HD = 128
KVH = 4
GROUPS = 4
SUF = 128
REQ_DEV = 3
TOK = 384
N_REQ = 32
PER = 12
TILE = 16
Y = 8
HALF = 64
SCALE = math.log2(math.e) / math.sqrt(HD)
NT = (((1,), (1,)), ((), ()))
MESH = pl.DeviceIdType.MESH
F32 = jnp.float32
BF16 = jnp.bfloat16
DOC = Y * 256
STEP = 256


def kernel(
    q_hbm, sk_hbm, sv_hbm, dk_hbm, dv_hbm, len_hbm, tgt_hbm, out_ref,
    q_ref, sk_ref, sv_ref, dk_ref, dv_ref, len_ref, tgt_ref,
    kv, vt, svt, s_ref, high, res, pick, unpick, send, recv,
    load_sem, ring_send, ring_recv, core_recv, ex_send, ex_recv,
):
    ctx, req = lax.axis_index("ctx"), lax.axis_index("req")
    y, xh = ctx // 2, ctx % 2
    z, quad = req // 4, req % 4
    xl, core = quad // 2, quad % 2
    steps = (0, 1, -1, 2, -2)

    def along(step, st):
        return ((y + step + Y) % Y) * 2 + (xh if st == 0 else 1 - xh)

    twin = req + 1 - 2 * core

    loads = [
        pltpu.make_async_copy(src, dst, load_sem.at[i])
        for i, (src, dst) in enumerate(
            (
                (dk_hbm, dk_ref), (dv_hbm, dv_ref), (tgt_hbm, tgt_ref), (len_hbm, len_ref),
                (q_hbm, q_ref), (sk_hbm, sk_ref), (sv_hbm, sv_ref),
            )
        )
    ]
    for load in loads:
        load.start()

    barrier = pltpu.get_barrier_semaphore()
    for st in range(2):
        for step in steps:
            if step != 0 or st != 0:
                pl.semaphore_signal(
                    barrier, inc=1, device_id=(along(step, st), req), device_id_type=MESH
                )

    @pl.loop(1, N_REQ)
    def _(s):
        pl.semaphore_signal(
            barrier, inc=1, device_id=(ctx, (req + s) % N_REQ), device_id_type=MESH
        )

    loads[0].wait()
    loads[1].wait()
    for g in range(KVH):
        lanes = slice(g * HD, (g + 1) * HD)
        for hf in range(2):
            start = core * HALF if hf == 0 else (1 - core) * HALF
            rows = pl.ds(pl.multiple_of(start, HALF), HALF)
            kv[0, g, 0, 0, hf] = dk_ref[rows, lanes]
            kv[1, g, 0, 0, hf] = dv_ref[rows, lanes]

    def ring(g, src, src_st, dst, st, other):
        pltpu.make_async_remote_copy(
            kv.at[:, g, src, src_st, 0], kv.at[:, g, dst, st, 0],
            ring_send.at[g], ring_recv.at[g, dst, st],
            device_id=(other, req), device_id_type=MESH,
        ).start()

    def pass_on(g, pos, st):
        pltpu.make_async_remote_copy(
            kv.at[:, g, pos, st, 0], kv.at[:, g, pos, st, 1],
            ring_send.at[g], core_recv.at[g, pos, st],
            device_id=(ctx, twin), device_id_type=MESH,
        ).start()

    def arrived(g, pos, st):
        part = kv.at[:, g, pos, st, 0]
        pltpu.make_async_copy(part, part, ring_recv.at[g, pos, st]).wait()

    def passed(g, pos, st):
        part = kv.at[:, g, pos, st, 1]
        pltpu.make_async_copy(part, part, core_recv.at[g, pos, st]).wait()

    def ring_start(g):
        for pos in (3, 4, 1, 2, 0):
            for st in range(2):
                if pos != 0 or st != 0:
                    ring(g, 0, 0, pos, st, along(steps[pos], st))

    def ring_relay(g):
        for st in range(2):
            arrived(g, 3, st)
            ring(g, 3, st, 5, st, along(1, 0))
            if st == 0:
                ring(g, 3, st, 7, st, along(2, 0))
            arrived(g, 4, st)
            ring(g, 4, st, 6, st, along(-1, 0))
            if st == 1:
                ring(g, 4, st, 7, st, along(-2, 0))
        for pos in range(5):
            for st in range(2):
                if pos in (1, 2) or (pos == 0 and st == 1):
                    arrived(g, pos, st)
                if pos != 0 or st != 0:
                    pass_on(g, pos, st)

    def ring_end(g):
        for pos in (5, 6, 7):
            for st in range(2):
                arrived(g, pos, st)
                pass_on(g, pos, st)

    def whole(g, first, last):
        for pos in range(first, last):
            for st in range(2):
                if pos > 0 or st > 0:
                    passed(g, pos, st)

    def query(g, hh):
        return q_ref[:, pl.ds(pl.multiple_of((g * GROUPS + hh) * HD, HD), HD)]

    lower = lax.broadcasted_iota(jnp.int32, (SUF, SUF), 0) <= lax.broadcasted_iota(
        jnp.int32, (SUF, SUF), 1
    )

    def key_lanes(g):
        return pl.ds(pl.multiple_of(g * HD, HD), HD)

    def suffix_scores(g, hh):
        q = query(g, hh)
        tops = []
        for r in range(REQ_DEV):
            rows = slice(r * SUF, (r + 1) * SUF)
            s = lax.dot_general(
                sk_ref[rows, key_lanes(g)], q[rows], NT, preferred_element_type=F32
            )
            s = jnp.where(lower, s, -jnp.inf)
            s_ref[hh, DOC:, rows] = s
            tops.append(jnp.max(s, axis=0, keepdims=True))
        return jnp.concatenate(tops, axis=1)

    def doc_scores(g, hh, first, last):
        n = (last - first) * 256
        keys = kv[0, g, first:last].reshape(n, HD)
        s = lax.dot_general(keys, query(g, hh), NT, preferred_element_type=F32)
        s_ref[hh, first * 256 : last * 256, :] = s
        return jnp.max(s, axis=0, keepdims=True)

    def turn(g, first, last):
        n = (last - first) * 256
        vt[:, first * 256 : last * 256] = kv[1, g, first:last].reshape(n, HD).T

    def attend(g, hh, top, ahead):
        total = summed = later = None
        for b in range(Y + 1):
            rows = slice(b * STEP, (b + 1) * STEP) if b < Y else slice(DOC, DOC + SUF)
            p = jnp.exp2((s_ref[hh, rows, :] - top) * SCALE)
            if ahead:
                t = doc_scores(g, hh + 1, b, b + 1) if b < Y else suffix_scores(g, hh + 1)
                later = t if later is None else jnp.maximum(later, t)
            t = jnp.sum(p, axis=0, keepdims=True)
            total = t if total is None else total + t
            p = p.astype(BF16)
            if b < Y:
                t = jnp.dot(vt[:, rows], p, preferred_element_type=F32)
            else:
                cols = [slice(r * SUF, (r + 1) * SUF) for r in range(REQ_DEV)]
                t = jnp.concatenate(
                    [jnp.dot(svt[:, c], p[:, c], preferred_element_type=F32) for c in cols], axis=1
                )
            summed = t if summed is None else summed + t
        o = summed * (1.0 / total)
        res[hh] = jnp.where(live > 0.0, o, 0.0).astype(BF16)
        return later

    for load in loads[2:4]:
        load.wait()
    lane = lax.broadcasted_iota(jnp.int32, (1, SUF), 1)
    live = jnp.concatenate([(lane < len_ref[r]).astype(F32) for r in range(REQ_DEV)], axis=1)

    def dispatch(g):
        for j in range(3):
            t = lax.dot_general(pick[0], res[j], NT, preferred_element_type=F32)
            t += lax.dot_general(pick[1 + j], res[3], NT, preferred_element_type=F32)
            send[g, :, j] = t.astype(BF16).reshape(N_REQ, TILE, HD)
        pltpu.make_async_copy(send.at[g, req], recv.at[g, req], ex_recv.at[g]).start()

        @pl.loop(0, N_REQ - 1)
        def _(s):
            j = s // 4
            step = (j // 2 + 1) * (1 - 2 * (j % 2)) + 4 * (j // 7)
            turned = s % 4 + s // 28
            x2, c2 = (xl + turned // 2) % 2, (core + turned) % 2
            dest = ((z + step + 8) % 8) * 4 + x2 * 2 + c2
            pltpu.make_async_remote_copy(
                send.at[g, dest], recv.at[g, req], ex_send.at[g], ex_recv.at[g],
                device_id=(ctx, dest), device_id_type=MESH,
            ).start()

    def collect(g):
        pltpu.make_async_copy(recv.at[g], recv.at[g], ex_recv.at[g]).wait()
        tiles = [recv[g, :, j].reshape(N_REQ * TILE, HD) for j in range(3)]
        last = None
        for j in range(3):
            lanes = slice((g * GROUPS + j) * HD, (g * GROUPS + j + 1) * HD)
            out_ref[:, lanes] = jnp.dot(unpick[0], tiles[j], preferred_element_type=F32).astype(BF16)
            t = jnp.dot(unpick[1 + j], tiles[j], preferred_element_type=F32)
            last = t if last is None else last + t
        out_ref[:, (g * GROUPS + 3) * HD : (g * GROUPS + 4) * HD] = last.astype(BF16)

    tgt = tgt_ref[...].reshape(1, TOK)
    mine = lax.broadcasted_iota(jnp.int32, (N_REQ, TOK), 0) == tgt
    before = lax.broadcasted_iota(jnp.int32, (TOK, TOK), 0) < lax.broadcasted_iota(
        jnp.int32, (TOK, TOK), 1
    )
    counts = jnp.dot(
        mine.astype(F32).astype(BF16), before.astype(F32).astype(BF16), preferred_element_type=F32
    )
    rank = jnp.sum(jnp.where(mine, counts, 0.0), axis=0, keepdims=True).astype(jnp.int32)
    row = lax.broadcasted_iota(jnp.int32, (N_REQ * TILE, TOK), 0)
    pick[0] = (row == tgt * TILE + rank).astype(F32).astype(BF16)
    spot = lax.broadcasted_iota(jnp.int32, (TOK, N_REQ * TILE), 1)
    place = lax.broadcasted_iota(jnp.int32, (TOK, N_REQ * TILE), 0)
    source, k = spot // TILE, spot % TILE
    unpick[0] = jnp.logical_and(place == source * PER + k, k < PER).astype(F32).astype(BF16)
    for j in range(3):
        inside = jnp.logical_and(rank >= 4 * j, rank < 4 * j + 4)
        code = jnp.where(inside, tgt * TILE + PER + rank - 4 * j, -1)
        pick[1 + j] = (row == code).astype(F32).astype(BF16)
        unpick[1 + j] = (
            jnp.logical_and(place == source * PER + 4 * j + k - PER, k >= PER)
            .astype(F32)
            .astype(BF16)
        )

    pl.semaphore_wait(barrier, N_REQ - 1 + 9)
    ring_start(0)
    for load in loads[4:]:
        load.wait()

    @pl.loop(0, GROUPS)
    def _(hh):
        high[hh] = suffix_scores(0, hh)

    ring_relay(0)
    ring_start(1)
    for first, last in ((0, 5), (5, Y)):
        if first > 0:
            ring_end(0)
        whole(0, first, last)
        turn(0, first, last)

        @pl.loop(0, GROUPS)
        def _(hh):
            high[hh] = jnp.maximum(high[hh], doc_scores(0, hh, first, last))

    def hooks(g, tick):
        def when(cond, act):
            if isinstance(g, int):
                if cond:
                    act()
            else:
                pl.when(cond)(act)

        if tick == 2:
            when(g + 1 < KVH, lambda: ring_relay(g + 1))
        if tick == 3:
            when(g + 2 < KVH, lambda: ring_start(g + 2))
        if tick == 4:
            when(g + 1 < KVH, lambda: ring_end(g + 1))

    svt[...] = sv_ref[:, 0:HD].T
    for hh in range(GROUPS):
        hooks(0, hh)
        attend(0, hh, high[hh], False)
    dispatch(0)
    hooks(0, 4)

    @pl.loop(1, KVH)
    def _(g):
        whole(g, 0, 8)
        turn(g, 0, 8)
        svt[...] = sv_ref[:, key_lanes(g)].T
        top = suffix_scores(g, 0)
        for b in range(Y):
            top = jnp.maximum(top, doc_scores(g, 0, b, b + 1))
        for hh in range(GROUPS):
            hooks(g, hh)
            top = attend(g, hh, top, hh < GROUPS - 1)
        dispatch(g)
        hooks(g, 4)

    for g in range(KVH):
        collect(g)
    for g in range(KVH):
        out = send.at[g, 0 : N_REQ - 1]
        pltpu.make_async_copy(out, out, ex_send.at[g]).wait()
        left = kv.at[:, 0:3, 0:5, :, 0]
        pltpu.make_async_copy(left, left, ring_send.at[g]).wait()


def body(queries, suffix_keys, suffix_values, doc_keys, doc_values, lengths, targets):
    vmem = pl.BlockSpec(memory_space=pltpu.VMEM)
    hbm = pl.BlockSpec(memory_space=pl.ANY)
    return pl.pallas_call(
        kernel,
        out_shape=jax.ShapeDtypeStruct((TOK, KVH * GROUPS * HD), BF16),
        in_specs=[hbm] * 7,
        out_specs=vmem,
        scratch_shapes=[
            pltpu.VMEM((TOK, KVH * GROUPS * HD), BF16),
            pltpu.VMEM((TOK, KVH * HD), BF16),
            pltpu.VMEM((TOK, KVH * HD), BF16),
            pltpu.VMEM((SUF, KVH * HD), BF16),
            pltpu.VMEM((SUF, KVH * HD), BF16),
            pltpu.SMEM((REQ_DEV,), jnp.int32),
            pltpu.VMEM((TOK,), jnp.int32),
            pltpu.VMEM((2, KVH, Y, 2, 2, HALF, HD), BF16),
            pltpu.VMEM((HD, DOC), BF16),
            pltpu.VMEM((HD, TOK), BF16),
            pltpu.VMEM((GROUPS, DOC + SUF, TOK), F32),
            pltpu.VMEM((GROUPS, 1, TOK), F32),
            pltpu.VMEM((GROUPS, HD, TOK), BF16),
            pltpu.VMEM((4, N_REQ * TILE, TOK), BF16),
            pltpu.VMEM((4, TOK, N_REQ * TILE), BF16),
            pltpu.VMEM((KVH, N_REQ, 3, TILE, HD), BF16),
            pltpu.VMEM((KVH, N_REQ, 3, TILE, HD), BF16),
            pltpu.SemaphoreType.DMA((7,)),
            pltpu.SemaphoreType.DMA((KVH,)),
            pltpu.SemaphoreType.DMA((KVH, Y, 2)),
            pltpu.SemaphoreType.DMA((KVH, Y, 2)),
            pltpu.SemaphoreType.DMA((KVH,)),
            pltpu.SemaphoreType.DMA((KVH,)),
        ],
        compiler_params=pltpu.CompilerParams(
            collective_id=0, has_side_effects=True, vmem_limit_bytes=56 << 20
        ),
        cost_estimate=pl.CostEstimate(
            flops=7_000_000_000, bytes_accessed=4_000_000, transcendentals=13_000_000
        ),
    )(queries, suffix_keys, suffix_values, doc_keys, doc_values, lengths, targets)


def solution(mesh):
    both = P(("ctx", "req"), None)
    flat = P(("ctx", "req"))
    in_specs = (both, both, both, P("ctx", None), P("ctx", None), flat, flat)
    return jax.shard_map(body, mesh=mesh, in_specs=in_specs, out_specs=both, check_vma=False)
```

time: 118 us -> 83.6 us (0.71)
  Pallas kernels: 109 us -> 80.7 us
  local copies, waits for them, and re-layouts: 7.69 us -> 2.73 us
    pallas_call x1, Pallas kernels: 109 us -> 80.7 us  [body(): pl.pallas_call(kernel, out_shape=jax.ShapeDtypeStruct((TOK, KVH * GROUPS...]
    unnamed x15 -> x1, local copies, waits for them, and re-layouts: 7.69 us -> 2.73 us
where the time goes in v2:
time: 83.6 us; the launch traced here: 83.4 us
  Pallas kernels  80.7 us (97%)
  local copies, waits for them, and re-layouts  2.73 us (3%)
    pallas_call x1, Pallas kernels, body(): pl.pallas_call(kernel, out_shape=jax.ShapeDtypeStruct((TOK, KVH * GROUPS...  80.7 us
    unnamed x1, local copies, waits for them, and re-layouts  2.73 us

profile of v2, /device:TPU:1, one launch (start us, length us, event | category | flops | bytes accessed | tf_op | source)
XLA Modules:
  0.0 83.4 jit_solution(18409974027194165975)
XLA Ops:
  0.0 80.7 %shard_map.73 = bf16[384,2048]{1,0:T(8,128)(2,1)} custom-call(bf16[384,2048]{1,0:T(8,128)(2,1)} %q_hbm.1, bf16[384,512]{1,0:T(8,128)(2,1)} %sk_hbm.1, bf16[384,512]{1,0:T(8,128)(2,1)} %sv_hbm.1, bf16[128,512]{1,0:T(8,128)(2,1)} %dk_hbm.1, bf16[128,512]{1,0:T(8,128)(2,1)} %dv_hbm.1, s32[3]{0:T(128)} %len_hbm.1, s32[384]{0:T(512)} %tgt_hbm.1), custom_call_target="tpu_custom_call" | custom-call | flops 7000000000 | bytes 4000000 | tf_op jit(solution)/shard_map/pallas_call | solution.py:326
  80.7 2.7 %copy.9 = bf16[384,2048]{1,0:T(8,128)(2,1)} copy(bf16[384,2048]{1,0:T(8,128)(2,1)} %shard_map.73) | data formatting | bytes 3145728

commit v3 on v2

--- a/solution.py
+++ b/solution.py
@@ -265,6 +265,7 @@
 
     ring_relay(0)
     ring_start(1)
+    ring_start(2)
     for first, last in ((0, 5), (5, Y)):
         if first > 0:
             ring_end(0)
@@ -283,10 +284,10 @@
             else:
                 pl.when(cond)(act)
 
-        if tick == 2:
+        if tick == 0:
             when(g + 1 < KVH, lambda: ring_relay(g + 1))
-        if tick == 3:
-            when(g + 2 < KVH, lambda: ring_start(g + 2))
+        if tick == 1:
+            when(g + 3 < KVH, lambda: ring_start(g + 3))
         if tick == 4:
             when(g + 1 < KVH, lambda: ring_end(g + 1))
 

time: 83.6 us -> 81.5 us (0.975)
  Pallas kernels: 80.7 us -> 77.9 us
    pallas_call x1, Pallas kernels: 80.7 us -> 77.9 us  [body(): pl.pallas_call(kernel, out_shape=jax.ShapeDtypeStruct((TOK, KVH * GROUPS...]
where the time goes in v3:
time: 81.5 us; the launch traced here: 80.6 us
  Pallas kernels  77.9 us (96%)
  local copies, waits for them, and re-layouts  2.73 us (3%)
    pallas_call x1, Pallas kernels, body(): pl.pallas_call(kernel, out_shape=jax.ShapeDtypeStruct((TOK, KVH * GROUPS...  77.9 us
    unnamed x1, local copies, waits for them, and re-layouts  2.73 us

profile of v3, /device:TPU:1, one launch (start us, length us, event | category | flops | bytes accessed | tf_op | source)
XLA Modules:
  0.0 80.6 jit_solution(4747519958387897232)
XLA Ops:
  0.0 77.9 %shard_map.73 = bf16[384,2048]{1,0:T(8,128)(2,1)} custom-call(bf16[384,2048]{1,0:T(8,128)(2,1)} %q_hbm.1, bf16[384,512]{1,0:T(8,128)(2,1)} %sk_hbm.1, bf16[384,512]{1,0:T(8,128)(2,1)} %sv_hbm.1, bf16[128,512]{1,0:T(8,128)(2,1)} %dk_hbm.1, bf16[128,512]{1,0:T(8,128)(2,1)} %dv_hbm.1, s32[3]{0:T(128)} %len_hbm.1, s32[384]{0:T(512)} %tgt_hbm.1), custom_call_target="tpu_custom_call" | custom-call | flops 7000000000 | bytes 4000000 | tf_op jit(solution)/shard_map/pallas_call | solution.py:327
  77.9 2.7 %copy.9 = bf16[384,2048]{1,0:T(8,128)(2,1)} copy(bf16[384,2048]{1,0:T(8,128)(2,1)} %shard_map.73) | data formatting | bytes 3145728
